TPU v7x, 128 devices: a whole 4x4x4 slice. The times are simulated.
128 devices in a mesh: ctx: 64 (over z_hi, y, x, core), head: 2 (over z_lo).
Axes of the slice: x: 4, y: 4, z: 4 (z_hi: 2, z_lo: 2; z = z_hi * 2 + z_lo), core: 2. Of those that a mesh axis runs over, the one named last changes fastest.
Arguments:
- q_heads: bfloat16 [128, 24576], P('ctx', 'head'), may hold values from -6 to 6
- w_uk: bfloat16 [128, 128, 512], P('head'), may hold values from -1 to 1
- latent_t: bfloat16 [576, 65536], P(None, 'ctx'), may hold values from -48 to 48
- index_query: bfloat16 [128, 8192], P('ctx', 'head'), may hold values from -48 to 48
- index_key: bfloat16 [65536, 128], P('ctx'), may hold values from -4 to 4
- head_weight: bfloat16 [128, 64], P('ctx', 'head'), may hold values from 0.099609375 to 1
- query_pos: int32 [128], replicated, may hold values from 32768 to 65535
- key_start: int32 [128], replicated, may hold values from 0 to 16383
Outputs:
- grad_index_query: float32 [128, 8192], P('ctx', 'head')
- grad_index_key: float32 [65536, 128], P('ctx')
- grad_head_weight: float32 [128, 64], P('ctx', 'head')
All inputs are finite; a program needn't handle non-finite values.
Results may differ from a plain program's by a relative error of at most 0.0035.
Values may be sent and summed in bfloat16 or wider, within the bound.
A program may use at most 192 MiB of HBM per device.

v0:
```python
import jax
import jax.numpy as jnp
from jax import lax
from jax.experimental import pallas as pl
from jax.experimental.pallas import tpu as pltpu
from jax.sharding import Mesh
from jax.sharding import PartitionSpec as P

NOPE = 128
ROPE = 64
IDIM = 128
CTX = ("zh", "y", "x", "c")
AXES = ("zh", "y", "x", "c", "head")
MESH_ID = pl.DeviceIdType.MESH

HEADS = 64
IHEADS = 32
QUERIES = 128
KEYS = 1024
ALL_KEYS = 65536
PAIRS = HEADS // 2
IPAIRS = IHEADS // 2
LOG2E = 1.4426950408889634
SCORE_K = (NOPE + ROPE) ** -0.5 * LOG2E
INDEX_SCALE = (IDIM * 64) ** -0.5
MASKED = -1.0e30
TCH = 256
CHUNKS = KEYS // TCH
BR = 80
NCOPY = 25

F32 = jnp.float32
BF16 = jnp.bfloat16


def nt(a, b):
    return lax.dot_general(a, b, (((1,), (1,)), ((), ())), preferred_element_type=F32)


def nn(a, b):
    return lax.dot_general(a, b, (((1,), (0,)), ((), ())), preferred_element_type=F32)


def body(
    blk, wuk, lat, key, bounds, rs_out, gk_out,
    g, nst, ost, wv, lext, lq, sc, pm, iqs, wt, ipart, irecv,
    st, r1, s2, r2, s3, r3, tpart, trecv, mis, keyt, gqt, gwt, gkp, gkr,
    rs, rcv, sb, rya, rxb, pa, pb, rxa, ryb, ab, rz,
    wsem, gsend, grecv, hsend, hrecv, tsend, trsem, ksend, krsem,
    s1send, s1recv, s2send, s2recv, s3send, s3recv, csend, crecv, ysend, yrecv, xsend, xrecv,
    x2send, x2recv, y2send, y2recv, zsend, zrecv,
):
    zh, y, x, c, hd = (lax.axis_index(a) for a in AXES)

    def at(zh_=None, y_=None, x_=None, c_=None, hd_=None):
        return (
            zh if zh_ is None else zh_, y if y_ is None else y_, x if x_ is None else x_,
            c if c_ is None else c_, hd if hd_ is None else hd_,
        )

    def remote(src, dst, ss, rsem, dev):
        return pltpu.make_async_remote_copy(
            src_ref=src, dst_ref=dst, send_sem=ss, recv_sem=rsem, device_id=dev, device_id_type=MESH_ID
        )

    g1, g2 = c * 4 + x, zh * 4 + y

    def peer1(k):
        p = lax.rem(g1 + k, 8)
        return p, at(x_=lax.rem(p, 4), c_=p // 4)

    def peer2(k):
        p = lax.rem(g2 + k, 8)
        return p, at(zh_=p // 4, y_=lax.rem(p, 4))

    barrier = pltpu.get_barrier_semaphore()
    for k in range(1, 8):
        pl.semaphore_signal(barrier, inc=1, device_id=peer1(k)[1], device_id_type=MESH_ID)
        pl.semaphore_signal(barrier, inc=1, device_id=peer2(k)[1], device_id_type=MESH_ID)
    pl.semaphore_signal(barrier, inc=1, device_id=at(hd_=1 - hd), device_id_type=MESH_ID)
    wcopy = pltpu.make_async_copy(wuk, wv, wsem)
    wcopy.start()
    g[c, y, x, zh] = blk[...]
    pl.semaphore_wait(barrier, 15)

    number = iter(range(NCOPY))

    def gcopy(ref, dev):
        k = next(number)
        cp = remote(ref, ref, gsend.at[k], grecv.at[k], dev)
        cp.start()
        return cp

    xr, xl = lax.rem(x + 1, 4), lax.rem(x + 3, 4)
    yr, yl = lax.rem(y + 1, 4), lax.rem(y + 3, 4)
    xo, yo = lax.rem(x + 2, 4), lax.rem(y + 2, 4)
    ra, rb = pl.ds(0, 128), pl.ds(128, 144)
    both, four = pl.ds(0, 2), pl.ds(0, 4)
    lo, hi = pl.ds(0, 2), pl.ds(2, 2)
    other = at(c_=1 - c)
    copies = []
    z0 = gcopy(g.at[c, y, x, zh], at(zh_=1 - zh))
    for a in range(4):
        lext[:, pl.ds(a * 128, 128)] = jnp.transpose(lat[pl.ds(a * 128, 128), :].astype(F32)).astype(BF16)
    rope = lat[pl.ds(512, 64), :].astype(F32)
    lext[:, pl.ds(512, 128)] = jnp.transpose(jnp.concatenate([rope, rope], axis=0)).astype(BF16)
    first = (((zh * 4 + y) * 4 + x) * 2 + c) * KEYS

    def seen(start, rows):
        ids = first + start + lax.broadcasted_iota(jnp.int32, (rows, QUERIES), 0)
        return (ids >= bounds[pl.ds(0, 1), :]) & (ids <= bounds[pl.ds(1, 1), :])

    lext[:, pl.ds(640, 128)] = jnp.where(seen(0, KEYS), 0.0, MASKED).astype(BF16)
    eye = (
        lax.broadcasted_iota(jnp.int32, (128, 128), 0) == lax.broadcasted_iota(jnp.int32, (128, 128), 1)
    ).astype(F32).astype(BF16)
    lq[pl.ds(0, 128), pl.ds(640, 128)] = eye
    lq[pl.ds(128, 128), pl.ds(640, 128)] = eye
    keyt[...] = jnp.transpose(key[...].astype(F32)).astype(BF16)
    z0.wait()
    a1 = gcopy(g.at[c, y, x, both, ra], at(x_=xr)), gcopy(g.at[c, y, x, both, ra], at(x_=xl))
    b1 = gcopy(g.at[c, y, x, both, rb], at(y_=yr)), gcopy(g.at[c, y, x, both, rb], at(y_=yl))
    a1[0].wait_recv()
    a2 = (gcopy(g.at[c, y, xl, 0, ra], at(x_=xr)),)
    b1[0].wait_recv()
    b2 = (gcopy(g.at[c, yl, x, 0, rb], at(y_=yr)),)
    a1[1].wait_recv()
    a2 += (gcopy(g.at[c, y, xr, 1, ra], at(x_=xl)),)
    b1[1].wait_recv()
    b2 += (gcopy(g.at[c, yr, x, 1, rb], at(y_=yl)),)
    a2[0].wait_recv()
    a2[1].wait_recv()
    a3 = (
        gcopy(g.at[c, y, four, both, ra], at(y_=yr)), gcopy(g.at[c, y, four, both, ra], at(y_=yl)),
    )
    copies += [gcopy(g.at[c, y, four, both, ra], other)]
    b2[0].wait_recv()
    b2[1].wait_recv()
    b3 = (
        gcopy(g.at[c, four, x, both, rb], at(x_=xr)), gcopy(g.at[c, four, x, both, rb], at(x_=xl)),
    )
    copies += [gcopy(g.at[c, four, x, both, rb], other)]
    a3[0].wait_recv()
    a4 = (gcopy(g.at[c, yl, lo, both, ra], at(y_=yr)),)
    copies += [gcopy(g.at[c, yl, four, both, ra], other)]
    b3[0].wait_recv()
    b4 = (gcopy(g.at[c, lo, xl, both, rb], at(x_=xr)),)
    copies += [gcopy(g.at[c, four, xl, both, rb], other)]
    a3[1].wait_recv()
    a4 += (gcopy(g.at[c, yr, hi, both, ra], at(y_=yl)),)
    copies += [gcopy(g.at[c, yr, four, both, ra], other)]
    b3[1].wait_recv()
    b4 += (gcopy(g.at[c, hi, xr, both, rb], at(x_=xl)),)
    copies += [gcopy(g.at[c, four, xr, both, rb], other)]
    a4[0].wait_recv()
    a4[1].wait_recv()
    copies += [gcopy(g.at[c, yo, four, both, ra], other)]
    b4[0].wait_recv()
    b4[1].wait_recv()
    copies += [gcopy(g.at[c, four, xo, both, rb], other)]
    for cp in copies:
        cp.wait()
    for cp in a1 + b1 + a2 + b2 + a3 + b3 + a4 + b4:
        cp.wait_send()

    def widen(o, _):
        oc, oy, ox, oz = o // 32, lax.rem(o // 8, 4), lax.rem(o // 2, 4), lax.rem(o, 2)
        nst[pl.ds(pl.multiple_of(o * 128, 128), 128), :] = g[oc, oy, ox, oz, pl.ds(0, 128), :].astype(F32)
        ost[pl.ds(pl.multiple_of(o * 144, 16), 144), :] = g[oc, oy, ox, oz, pl.ds(128, 144), :].astype(F32)
        return 0

    lax.fori_loop(0, 64, widen, 0)

    def rows_of(ref, offset, step, stride):
        return jnp.concatenate(
            [ref[pl.ds(offset + r * step, 64, stride=stride), :] for r in range(2)], axis=0
        )

    wt[...] = jnp.transpose(rows_of(ost, 128, 1, 144)) * INDEX_SCALE

    ipart[...] = jnp.zeros_like(ipart)

    def index_pair(jp, _):
        for e in range(2):
            iqs[jp, pl.ds(e * 128, 128), :] = rows_of(ost, 64 + 2 * jp + e, 32, 144).astype(BF16)
        d = jnp.maximum(nt(key[...], iqs[jp]), 0.0)
        w0, w1 = wt[pl.ds(2 * jp, 1), :], wt[pl.ds(2 * jp + 1, 1), :]
        ipart[...] += d[:, :128] * w0 + d[:, 128:] * w1
        return 0

    lax.fori_loop(0, IPAIRS, index_pair, 0)
    hcopy = remote(ipart, irecv, hsend, hrecv, at(hd_=1 - hd))
    hcopy.start()

    wcopy.wait()
    half = lax.broadcasted_iota(jnp.int32, (128, 128), 1) // 64

    def score_pair(p, _):
        rp = rows_of(ost, p, 32, 144)
        for e in range(2):
            qn = rows_of(nst, 2 * p + e, 64, 128).astype(BF16)
            lq[pl.ds(e * 128, 128), pl.ds(0, 512)] = nn(qn, wv[2 * p + e]).astype(BF16)
            lq[pl.ds(e * 128, 128), pl.ds(512, 128)] = jnp.where(half == e, rp, 0.0).astype(BF16)
        sc[...] = nt(lext[...], lq[...]) * SCORE_K
        t = sc[...]
        m = jnp.max(t, axis=0, keepdims=True)
        pw = jnp.exp2(t - m)
        l = jnp.sum(pw, axis=0, keepdims=True)
        pm[p] = pw.astype(BF16)
        gi, row = p // 4, lax.rem(p, 4) * 2
        for e in range(2):
            st[gi, pl.ds(row + e, 1), :] = m[:, e * 128 : e * 128 + 128]
            st[gi, pl.ds(8 + row + e, 1), :] = l[:, e * 128 : e * 128 + 128]
        return 0

    lax.fori_loop(0, PAIRS, score_pair, 0)

    hcopy.wait()
    it = jnp.where(seen(0, KEYS), (ipart[...] + irecv[...]) * LOG2E, MASKED)
    im = jnp.max(it, axis=0, keepdims=True)
    il = jnp.sum(jnp.exp2(it - im), axis=0, keepdims=True)
    mis[...] = it
    for gi in range(8):
        st[gi, pl.ds(16, 1), :] = im
        st[gi, pl.ds(17, 1), :] = il

    def merged(ref):
        mm = ref[0, pl.ds(0, 8), :]
        jm = ref[0, pl.ds(16, 1), :]
        for k in range(1, 8):
            mm = jnp.maximum(mm, ref[k, pl.ds(0, 8), :])
            jm = jnp.maximum(jm, ref[k, pl.ds(16, 1), :])
        ll, jl = jnp.zeros_like(mm), jnp.zeros_like(jm)
        for k in range(8):
            ll += ref[k, pl.ds(8, 8), :] * jnp.exp2(ref[k, pl.ds(0, 8), :] - mm)
            jl += ref[k, pl.ds(17, 1), :] * jnp.exp2(ref[k, pl.ds(16, 1), :] - jm)
        return mm, ll, jm, jl

    def put(ref, values):
        for at_row, rows, v in zip((0, 8, 16, 17), (8, 8, 1, 1), values):
            ref[pl.ds(at_row, rows), :] = v

    def swap(copies):
        for cp in copies:
            cp.start()
        for cp in copies:
            cp.wait()

    r1[g1] = st[g1]
    cps = []
    for k in range(1, 8):
        p, dev = peer1(k)
        cps.append(remote(st.at[p], r1.at[g1], s1send.at[k], s1recv.at[k], dev))
    swap(cps)
    put(s2, merged(r1))
    r2[g2] = s2[...]
    cps = []
    for k in range(1, 8):
        p, dev = peer2(k)
        cps.append(remote(s2, r2.at[g2], s2send.at[k], s2recv.at[k], dev))
    swap(cps)
    put(s3, merged(r2))
    r3[g1] = s3[...]
    cps = []
    for k in range(1, 8):
        p, dev = peer1(k)
        cps.append(remote(s3, r3.at[g1], s3send.at[k], s3recv.at[k], dev))
    swap(cps)
    for gi in range(8):
        st[gi, pl.ds(0, 8), :] = jnp.exp2(st[gi, pl.ds(0, 8), :] - r3[gi, pl.ds(0, 8), :]) / (
            r3[gi, pl.ds(8, 8), :] * 128.0
        )
    jpeak, jtotal = s3[pl.ds(16, 1), :], s3[pl.ds(17, 1), :]

    tcopies = []
    for ch in range(CHUNKS):
        def add_group(gi, acc, ch=ch):
            for a in range(4):
                pw = pm[gi * 4 + a, pl.ds(ch * TCH, TCH), :].astype(F32)
                acc = acc + pw[:, :128] * st[gi, pl.ds(2 * a, 1), :] + pw[:, 128:] * st[gi, pl.ds(2 * a + 1, 1), :]
            return acc

        rows = pl.ds(ch * TCH, TCH)
        tpart[rows, :] = lax.fori_loop(0, 8, add_group, jnp.zeros((TCH, QUERIES), F32))
        cp = remote(tpart.at[rows], trecv.at[rows], tsend.at[ch], trsem.at[ch], at(hd_=1 - hd))
        cp.start()
        tcopies.append(cp)

    gqt[...] = jnp.zeros_like(gqt)
    gwt[...] = jnp.zeros_like(gwt)
    kcopies = []
    for ch in range(CHUNKS):
        rows = pl.ds(ch * TCH, TCH)
        tcopies[ch].wait()
        predicted = jnp.exp2(mis[rows, :] - jpeak) / jtotal
        mis[rows, :] = (predicted - (tpart[rows, :] + trecv[rows, :])) * ALL_KEYS

        def slope_pair(jp, acc, rows=rows):
            iq = iqs[jp]
            mf = mis[rows, :]
            d = nt(key[rows, :], iq)
            parts = []
            for e in range(2):
                de = d[:, e * 128 : e * 128 + 128]
                gwt[pl.ds(2 * jp + e, 1), :] += jnp.sum(mf * jnp.maximum(de, 0.0), axis=0, keepdims=True)
                parts.append(jnp.where(de > 0, mf * wt[pl.ds(2 * jp + e, 1), :], 0.0).astype(BF16))
            sl = jnp.concatenate(parts, axis=1)
            gqt[jp] += nn(keyt[:, rows], sl)
            return acc + nn(sl, iq)

        gkp[rows, :] = lax.fori_loop(0, IPAIRS, slope_pair, jnp.zeros((TCH, IDIM), F32))
        cp = remote(gkp.at[rows], gkr.at[rows], ksend.at[ch], krsem.at[ch], at(hd_=1 - hd))
        cp.start()
        kcopies.append(cp)

    for j in range(IHEADS):
        tr = jnp.transpose(gqt[j // 2, :, pl.ds((j % 2) * 128, 128)])
        for r in range(2):
            rs[pl.ds(r * 32 + j, 64, stride=BR), :] = tr[r * 64 : r * 64 + 64]
    tw = jnp.transpose(gwt[...]) * INDEX_SCALE
    for r in range(16):
        rs[pl.ds(64 + r, 64, stride=BR), :] = tw[r * 64 : r * 64 + 64] if r < 2 else jnp.zeros((64, 128), F32)

    ccopy = remote(
        rs.at[pl.ds(pl.multiple_of((1 - c) * 32 * BR, BR), 32 * BR)], rcv, csend, crecv, other
    )
    ccopy.start()
    ccopy.wait()

    def add_core(o, _):
        oy, ox, oz = o // 8, lax.rem(o // 2, 4), lax.rem(o, 2)
        here = pl.ds(pl.multiple_of(o * BR, BR), BR)
        v = rcv[here, :] + rs[pl.ds(pl.multiple_of((c * 32 + o) * BR, BR), BR), :]
        rcv[here, :] = v
        w = v[64:72]
        low = w - w.astype(BF16).astype(F32)
        sb[oy, ox, oz] = jnp.concatenate([v[:72], low], axis=0).astype(BF16)
        return 0

    lax.fori_loop(0, 32, add_core, 0)
    cps = []
    for k in range(1, 4):
        yp, xp = lax.rem(y + k, 4), lax.rem(x + k, 4)
        cps.append(remote(sb.at[yp, four, 0], rya.at[k], ysend.at[k], yrecv.at[k], at(y_=yp)))
        cps.append(remote(sb.at[four, xp, 1], rxb.at[k], xsend.at[k], xrecv.at[k], at(x_=xp)))
    swap(cps)

    for o in range(4):
        for dest, src, index in (
            (pa, rya, (y * 4 + o) * 2),
            (pb, rxb, (o * 4 + x) * 2 + 1),
        ):
            v = rcv[pl.ds(pl.multiple_of(index * BR, BR), BR), :]
            main, w = v[:64], v[64:72]
            for k in range(1, 4):
                vk = src[k, o].astype(F32)
                main, w = main + vk[:64], w + (vk[64:72] + vk[72:])
            dest[o, pl.ds(0, 64), :] = main
            dest[o, pl.ds(64, 8), :] = w
            dest[o, pl.ds(72, 8), :] = jnp.zeros((8, 128), F32)
    cps = []
    for k in range(1, 4):
        yp, xp = lax.rem(y + k, 4), lax.rem(x + k, 4)
        cps.append(remote(pa.at[xp], rxa.at[k], x2send.at[k], x2recv.at[k], at(x_=xp)))
        cps.append(remote(pb.at[yp], ryb.at[k], y2send.at[k], y2recv.at[k], at(y_=yp)))
    swap(cps)
    ab[0] = pa[x] + rxa[1] + rxa[2] + rxa[3]
    ab[1] = pb[y] + ryb[1] + ryb[2] + ryb[3]
    swap([remote(ab.at[1 - zh], rz, zsend, zrecv, at(zh_=1 - zh))])
    rs_out[...] = ab[zh] + rz[...]
    for cp in kcopies:
        cp.wait()
    gk_out[...] = gkp[...] + gkr[...]


def shards(q_heads, w_uk, latent_t, index_query, index_key, head_weight, query_pos, key_start):
    shaped = q_heads.reshape(2, HEADS, NOPE + ROPE)
    blk = jnp.concatenate(
        [
            shaped[:, :, :NOPE].reshape(2 * HEADS, 128),
            shaped[:, :, NOPE:].reshape(HEADS, 128),
            index_query.reshape(2 * IHEADS, IDIM),
            jnp.pad(head_weight, ((0, 14), (0, 128 - IHEADS))),
        ],
        axis=0,
    )

    def ordered(v):
        return v.reshape(2, 4, 4, 2, 2).transpose(4, 3, 1, 2, 0).reshape(1, QUERIES)

    bounds = jnp.pad(jnp.concatenate([ordered(key_start), ordered(query_pos)], axis=0), ((0, 6), (0, 0)))
    vm = pl.BlockSpec(memory_space=pltpu.VMEM)
    dma = pltpu.SemaphoreType.DMA

    def v(*shape, dtype=F32):
        return pltpu.VMEM(shape, dtype)

    rs, gk = pl.pallas_call(
        body,
        out_shape=(jax.ShapeDtypeStruct((BR, 128), F32), jax.ShapeDtypeStruct((KEYS, IDIM), F32)),
        in_specs=[vm, pl.BlockSpec(memory_space=pl.ANY), vm, vm, vm],
        out_specs=(vm, vm),
        scratch_shapes=[
            v(2, 4, 4, 2, 272, 128, dtype=BF16),
            v(64 * 128, 128),
            v(64 * 144, 128),
            v(HEADS, NOPE, 512, dtype=BF16),
            v(KEYS, 768, dtype=BF16),
            v(256, 768, dtype=BF16),
            v(KEYS, 256),
            v(PAIRS, KEYS, 256, dtype=BF16),
            v(IPAIRS, 256, 128, dtype=BF16),
            v(128, 128),
            v(KEYS, 128),
            v(KEYS, 128),
            v(8, 24, 128),
            v(8, 24, 128),
            v(24, 128),
            v(8, 24, 128),
            v(24, 128),
            v(8, 24, 128),
            v(KEYS, 128),
            v(KEYS, 128),
            v(KEYS, 128),
            v(128, KEYS, dtype=BF16),
            v(IPAIRS, 128, 256),
            v(128, 128),
            v(KEYS, 128),
            v(KEYS, 128),
            v(64 * BR, 128),
            v(32 * BR, 128),
            v(4, 4, 2, BR, 128, dtype=BF16),
            v(4, 4, BR, 128, dtype=BF16),
            v(4, 4, BR, 128, dtype=BF16),
            v(4, BR, 128),
            v(4, BR, 128),
            v(4, BR, 128),
            v(4, BR, 128),
            v(2, BR, 128),
            v(BR, 128),
            dma, dma((NCOPY,)), dma((NCOPY,)), dma, dma,
            dma((CHUNKS,)), dma((CHUNKS,)), dma((CHUNKS,)), dma((CHUNKS,)),
            dma((8,)), dma((8,)), dma((8,)), dma((8,)), dma((8,)), dma((8,)),
            dma, dma, dma((4,)), dma((4,)), dma((4,)), dma((4,)),
            dma((4,)), dma((4,)), dma((4,)), dma((4,)), dma, dma,
        ],
        compiler_params=pltpu.CompilerParams(
            collective_id=0, has_side_effects=True, vmem_limit_bytes=63 * 1024 * 1024
        ),
    )(blk, w_uk, latent_t, index_key, bounds)
    grad_query = rs[:64].reshape(2, IHEADS * IDIM)
    grad_weight = rs[64:66, :IHEADS]
    return grad_query, gk, grad_weight


def solution(mesh):
    torus = Mesh(mesh.devices.reshape(2, 4, 4, 2, 2), AXES)
    placed = (
        P(CTX, "head"),
        P("head", None, None),
        P(None, CTX),
        P(CTX, "head"),
        P(CTX, None),
        P(CTX, "head"),
        P(),
        P(),
    )
    return jax.shard_map(
        shards,
        mesh=torus,
        in_specs=placed,
        out_specs=(P(CTX, "head"), P(CTX, None), P(CTX, "head")),
        check_vma=False,
    )
```

profile of v0, /device:TPU:0, one launch (start us, length us, event | category | flops | bytes accessed | tf_op | source)
XLA Modules:
  0.0 156.0 jit_solution(7876138812275650207)
XLA Ops:
  0.6 0.9 reshape.33
  1.5 0.1 reshape.35
  1.6 0.7 reshape.36
  2.4 1.3 fusion.1.blk
  3.7 0.8 reshape.37
  4.5 0.3 copy.13
  4.8 0.2 reshape.38
  5.0 0.8 reshape.39
  5.8 0.3 copy.14
  6.1 0.2 reshape.40
  6.3 0.6 pad.9.bounds
  6.9 144.6 %shard_map.103 = (f32[80,128]{1,0:T(8,128)}, f32[1024,128]{1,0:T(8,128)}) custom-call(bf16[272,128]{1,0:T(8,128)(2,1)} %fusion.1.blk, bf16[64,128,512]{2,1,0:T(8,128)(2,1)} %wuk.1, bf16[576,1024]{1,0:T(8,128)(2,1)} %lat.1, bf16[1024,128]{1,0:T(8,128)(2,1)} %key.1, s32[8,128]{1,0:T(8,128)} %pad.9.bounds), custom_call_target="tpu_custom_call" | custom-call | tf_op jit(solution)/shard_map/pallas_call | solution.py:398
  151.5 0.8 slice.14
  152.2 0.6 reshape.41
  152.9 1.2 slice.15
  154.1 1.9 %copy.16 = f32[1024,128]{1,0:T(8,128)} copy(f32[1024,128]{1,0:T(8,128)} %get-tuple-element.11) | data formatting | bytes 1048576
  (3 shorter events, 0.0 us)
where the time goes:
time: 156 us
  Pallas kernels  145 us (93%)
  local copies, waits for them, and re-layouts  9.4 us (6%)
    pallas_call x1, Pallas kernels, shards(): pl.pallas_call(body, out_shape=(jax.ShapeDtypeStruct((BR, 128), F32), jax...  145 us

commit v1 on v0

v1 whole, which is shorter than its diff:
```python
import jax
import jax.numpy as jnp
from jax import lax
from jax.experimental import pallas as pl
from jax.experimental.pallas import tpu as pltpu
from jax.sharding import Mesh
from jax.sharding import PartitionSpec as P

NOPE = 128
ROPE = 64
IDIM = 128
CTX = ("zh", "y", "x", "c")
AXES = ("zh", "y", "x", "c", "head")
MESH_ID = pl.DeviceIdType.MESH

HEADS = 64
IHEADS = 32
QUERIES = 128
KEYS = 1024
ALL_KEYS = 65536
PAIRS = HEADS // 2
IPAIRS = IHEADS // 2
LOG2E = 1.4426950408889634
SCORE_K = (NOPE + ROPE) ** -0.5 * LOG2E
INDEX_SCALE = (IDIM * 64) ** -0.5
MASKED = -1.0e30
TCH = 256
CHUNKS = KEYS // TCH
BR = 80
NCOPY = 75
UNR = 4
SCH = 256

F32 = jnp.float32
BF16 = jnp.bfloat16


def nt(a, b):
    return lax.dot_general(a, b, (((1,), (1,)), ((), ())), preferred_element_type=F32)


def nn(a, b):
    return lax.dot_general(a, b, (((1,), (0,)), ((), ())), preferred_element_type=F32)


def body(
    qh, iqh, hw, start_in, pos_in, wuk, lat, key, gq_out, gk_out, gw_out,
    raw, low, high, g, hst, ist, wv, lext, lq, lq2, sc, sc2, pm, iqs, wt, ipart, irecv,
    st, r1, s2, r2, s3, r3, tpart, trecv, mis, keyt, gqt, gwt, gkp, gkr,
    rs, rcv, sb, rya, rxb, pab, rz,
    wsem, gsend, grecv, hsend, hrecv, tsend, trsem, ksend, krsem,
    s1send, s1recv, s2send, s2recv, s3send, s3recv, csend, crecv, ysend, yrecv, xsend, xrecv,
    zsend, zrecv,
):
    zh, y, x, c, hd = (lax.axis_index(a) for a in AXES)

    def at(zh_=None, y_=None, x_=None, c_=None, hd_=None):
        return (
            zh if zh_ is None else zh_, y if y_ is None else y_, x if x_ is None else x_,
            c if c_ is None else c_, hd if hd_ is None else hd_,
        )

    def remote(src, dst, ss, rsem, dev):
        return pltpu.make_async_remote_copy(
            src_ref=src, dst_ref=dst, send_sem=ss, recv_sem=rsem, device_id=dev, device_id_type=MESH_ID
        )

    g1, g2 = c * 4 + x, zh * 4 + y

    def peer1(k):
        p = lax.rem(g1 + k, 8)
        return p, at(x_=lax.rem(p, 4), c_=p // 4)

    def peer2(k):
        p = lax.rem(g2 + k, 8)
        return p, at(zh_=p // 4, y_=lax.rem(p, 4))

    barrier = pltpu.get_barrier_semaphore()
    for k in range(1, 8):
        pl.semaphore_signal(barrier, inc=1, device_id=peer1(k)[1], device_id_type=MESH_ID)
        pl.semaphore_signal(barrier, inc=1, device_id=peer2(k)[1], device_id_type=MESH_ID)
    pl.semaphore_signal(barrier, inc=1, device_id=at(hd_=1 - hd), device_id_type=MESH_ID)
    for k in range(1, 4):
        pl.semaphore_signal(
            barrier, inc=1, device_id=at(zh_=1 - zh, x_=lax.rem(x + k, 4)), device_id_type=MESH_ID
        )
    wcopy = pltpu.make_async_copy(wuk, wv, wsem)
    wcopy.start()

    lane = lax.broadcasted_iota(jnp.int32, (2, 128), 1)
    raw[pl.ds(64, 16), :] = jnp.zeros((16, 128), F32)
    for r in range(2):
        raw[pl.ds(64 + r, 1), pl.ds(0, IHEADS)] = hw[pl.ds(r, 1), :].astype(F32)
    for j in range(IHEADS):
        t = iqh[:, pl.ds(j * 128, 128)].astype(F32)
        for r in range(2):
            raw[pl.ds(r * 32 + j, 1), :] = t[r : r + 1]
    for p in range(PAIRS):
        t0, t1, t2 = (qh[:, pl.ds(p * 384 + a * 128, 128)].astype(F32) for a in range(3))
        rope = jnp.where(lane < 64, t1, t2)
        second = pltpu.roll(jnp.where(lane < 64, t2, t1), 64, 1)
        base = 80 + (p // 16) * 96
        hl, pr = (p % 16) * 2, p % 16
        for r in range(2):
            raw[pl.ds(base + r * 32 + hl, 1), :] = t0[r : r + 1]
            raw[pl.ds(base + r * 32 + hl + 1, 1), :] = second[r : r + 1]
            raw[pl.ds(base + 64 + r * 16 + pr, 1), :] = rope[r : r + 1]
    g[c, y, x, zh] = raw[...].astype(BF16)
    qa = lax.broadcasted_iota(jnp.int32, (128, 128), 0)
    qb = lax.broadcasted_iota(jnp.int32, (128, 128), 1)
    place = (
        lax.rem(qb, 2) * 64 + lax.rem(qb // 8, 4) * 16 + lax.rem(qb // 2, 4) * 4 + lax.rem(qb // 32, 2) * 2 + qb // 64
    )
    moved = (qa == place).astype(F32).astype(BF16)

    def ordered(ref):
        v = jnp.broadcast_to(ref[...], (8, 128))
        top = nn((v // 256).astype(F32).astype(BF16), moved)
        rest = nn(lax.rem(v, 256).astype(F32).astype(BF16), moved)
        return (top * 256.0 + rest).astype(jnp.int32)

    low[...] = ordered(start_in)
    high[...] = ordered(pos_in)
    pl.semaphore_wait(barrier, 18)

    number = iter(range(NCOPY))

    def gcopy(ref, dev):
        k = next(number)
        return remote(ref, ref, gsend.at[k], grecv.at[k], dev)

    xr, xl = lax.rem(x + 1, 4), lax.rem(x + 3, 4)
    yr, yl = lax.rem(y + 1, 4), lax.rem(y + 3, 4)
    xo, yo = lax.rem(x + 2, 4), lax.rem(y + 2, 4)
    both, four = pl.ds(0, 2), pl.ds(0, 4)
    front, back = pl.ds(0, 2), pl.ds(2, 2)
    dxr, dxl, dyr, dyl = at(x_=xr), at(x_=xl), at(y_=yr), at(y_=yl)
    other, across = at(c_=1 - c), at(zh_=1 - zh)

    class Piece:
        def __init__(self, row, na, nb):
            ra, rb = pl.ds(row, na), pl.ds(row + na, nb)
            self.z = gcopy(g.at[c, y, x, zh, pl.ds(row, na + nb)], across)
            self.a1 = [gcopy(g.at[c, y, x, both, ra], d) for d in (dxr, dxl)]
            self.b1 = [gcopy(g.at[c, y, x, both, rb], d) for d in (dyr, dyl)]
            self.a2 = [gcopy(g.at[c, y, xl, 0, ra], dxr), gcopy(g.at[c, y, xr, 1, ra], dxl)]
            self.b2 = [gcopy(g.at[c, yl, x, 0, rb], dyr), gcopy(g.at[c, yr, x, 1, rb], dyl)]
            self.a3 = [gcopy(g.at[c, y, four, both, ra], d) for d in (dyr, dyl)]
            self.b3 = [gcopy(g.at[c, four, x, both, rb], d) for d in (dxr, dxl)]
            self.a4 = [gcopy(g.at[c, yl, front, both, ra], dyr), gcopy(g.at[c, yr, back, both, ra], dyl)]
            self.b4 = [gcopy(g.at[c, front, xl, both, rb], dxr), gcopy(g.at[c, back, xr, both, rb], dxl)]
            self.ca = [gcopy(g.at[c, yy, four, both, ra], other) for yy in (y, yl, yr, yo)]
            self.cb = [gcopy(g.at[c, four, xx, both, rb], other) for xx in (x, xl, xr, xo)]

        def step1(self):
            self.z.start()

        def step2(self):
            self.z.wait_recv()
            for cp in self.a1 + self.b1:
                cp.start()

        def step3(self):
            for k in range(2):
                for before, after in ((self.a1, self.a2), (self.b1, self.b2)):
                    before[k].wait_recv()
                    after[k].start()

        def step4(self):
            for before, after, core in ((self.a2, self.a3, self.ca), (self.b2, self.b3, self.cb)):
                for cp in before:
                    cp.wait_recv()
                for cp in after:
                    cp.start()
                core[0].start()

        def step5(self):
            for k in range(2):
                for before, after, core in ((self.a3, self.a4, self.ca), (self.b3, self.b4, self.cb)):
                    before[k].wait_recv()
                    after[k].start()
                    core[1 + k].start()

        def step6(self):
            for before, core in ((self.a4, self.ca), (self.b4, self.cb)):
                for cp in before:
                    cp.wait_recv()
                core[3].start()

        def step7(self):
            for cp in self.ca + self.cb:
                cp.wait()
            for cp in [self.z] + self.a1 + self.b1 + self.a2 + self.b2 + self.a3 + self.b3 + self.a4 + self.b4:
                cp.wait_send()

    first = (((zh * 4 + y) * 4 + x) * 2 + c) * KEYS

    def seen():
        ids = first + lax.broadcasted_iota(jnp.int32, (KEYS, QUERIES), 0)
        return (ids >= low[pl.ds(0, 1), :]) & (ids <= high[pl.ds(0, 1), :])

    def turn(a):
        lext[:, pl.ds(a * 128, 128)] = jnp.transpose(lat[pl.ds(a * 128, 128), :].astype(F32)).astype(BF16)

    p0, p1, p2 = Piece(0, 32, 48), Piece(80, 48, 48), Piece(176, 48, 48)
    p0.step1()
    p1.step1()
    p2.step1()
    lext[:, pl.ds(640, 128)] = jnp.where(seen(), 0.0, MASKED).astype(BF16)
    p0.step2()
    eye = (qa == qb).astype(F32).astype(BF16)
    for ref in (lq, lq2):
        ref[pl.ds(0, 128), pl.ds(640, 128)] = eye
        ref[pl.ds(128, 128), pl.ds(640, 128)] = eye
    p1.step2()
    turn(0)
    p0.step3()
    p2.step2()
    turn(1)
    p0.step4()
    p1.step3()
    turn(2)
    p2.step3()
    p0.step5()
    p1.step4()
    turn(3)
    rope_rows = lat[pl.ds(512, 64), :].astype(F32)
    lext[:, pl.ds(512, 128)] = jnp.transpose(jnp.concatenate([rope_rows, rope_rows], axis=0)).astype(BF16)
    keyt[...] = jnp.transpose(key[...].astype(F32)).astype(BF16)
    p0.step6()
    p0.step7()

    def widened(dest, base, row, rows):
        def one(o, _):
            oc, oy, ox, oz = o // 32, lax.rem(o // 8, 4), lax.rem(o // 2, 4), lax.rem(o, 2)
            dest[pl.ds(pl.multiple_of(base + o * rows, 16), rows), :] = g[oc, oy, ox, oz, pl.ds(row, rows), :].astype(F32)
            return 0

        lax.fori_loop(0, 64, one, 0)

    def rows_of(ref, offset, step, stride):
        return jnp.concatenate(
            [ref[pl.ds(offset + r * step, 64, stride=stride), :] for r in range(2)], axis=0
        )

    widened(ist, 0, 0, 80)
    wt[...] = jnp.transpose(rows_of(ist, 64, 1, 80)) * INDEX_SCALE

    ipart[...] = jnp.zeros_like(ipart)

    def index_pair(jp, _):
        for e in range(2):
            iqs[jp, pl.ds(e * 128, 128), :] = rows_of(ist, 2 * jp + e, 32, 80).astype(BF16)
        d = jnp.maximum(nt(key[...], iqs[jp]), 0.0)
        w0, w1 = wt[pl.ds(2 * jp, 1), :], wt[pl.ds(2 * jp + 1, 1), :]
        ipart[...] += d[:, :128] * w0 + d[:, 128:] * w1
        return 0

    lax.fori_loop(0, IPAIRS // 2, index_pair, 0, unroll=2)
    p1.step5()
    p2.step4()
    lax.fori_loop(IPAIRS // 2, IPAIRS, index_pair, 0, unroll=2)
    hcopy = remote(ipart, irecv, hsend, hrecv, at(hd_=1 - hd))
    hcopy.start()
    p1.step6()
    p2.step5()
    p1.step7()
    widened(hst, 0, 80, 96)

    wcopy.wait()
    half = lax.broadcasted_iota(jnp.int32, (128, 128), 1) // 64

    def prepare(p, dest):
        base = (p // 16) * 6144
        pr = lax.rem(p, 16)
        rp = rows_of(hst, base + 64 + pr, 16, 96)
        for e in range(2):
            qn = rows_of(hst, base + pr * 2 + e, 32, 96).astype(BF16)
            dest[pl.ds(e * 128, 128), pl.ds(0, 512)] = nn(qn, wv[2 * p + e]).astype(BF16)
            dest[pl.ds(e * 128, 128), pl.ds(512, 128)] = jnp.where(half == e, rp, 0.0).astype(BF16)

    def scores(src, dest):
        peak = None
        for a in range(KEYS // SCH):
            t = nt(lext[pl.ds(a * SCH, SCH), :], src[...])
            dest[pl.ds(a * SCH, SCH), :] = t
            top = jnp.max(t.reshape(SCH // 8, 8, 256), axis=0)
            peak = top if peak is None else jnp.maximum(peak, top)
        return jnp.max(peak, axis=0, keepdims=True)

    def powers(p, src, peak):
        total = None
        for a in range(KEYS // SCH):
            pw = jnp.exp2((src[pl.ds(a * SCH, SCH), :] - peak) * SCORE_K)
            pm[p, pl.ds(a * SCH, SCH), :] = pw.astype(BF16)
            part = jnp.sum(pw.reshape(SCH // 8, 8, 256), axis=0)
            total = part if total is None else total + part
        l = jnp.sum(total, axis=0, keepdims=True)
        m = peak * SCORE_K
        part, gi, row = p // 16, lax.rem(p, 16) // 2, lax.rem(p, 2) * 2
        for e in range(2):
            st[part, gi, pl.ds(row + e, 1), :] = m[:, e * 128 : e * 128 + 128]
            st[part, gi, pl.ds(4 + row + e, 1), :] = l[:, e * 128 : e * 128 + 128]

    def merged(ref, part):
        mm = ref[part, 0, pl.ds(0, 4), :]
        jm = ref[part, 0, pl.ds(8, 1), :]
        for k in range(1, 8):
            mm = jnp.maximum(mm, ref[part, k, pl.ds(0, 4), :])
            jm = jnp.maximum(jm, ref[part, k, pl.ds(8, 1), :])
        ll, jl = jnp.zeros_like(mm), jnp.zeros_like(jm)
        for k in range(8):
            ll += ref[part, k, pl.ds(4, 4), :] * jnp.exp2(ref[part, k, pl.ds(0, 4), :] - mm)
            jl += ref[part, k, pl.ds(9, 1), :] * jnp.exp2(ref[part, k, pl.ds(8, 1), :] - jm)
        return mm, ll, jm, jl

    def put(ref, part, values):
        for at_row, rows, v in zip((0, 4, 8, 9), (4, 4, 1, 1), values):
            ref[part, pl.ds(at_row, rows), :] = v

    def begin(copies):
        for cp in copies:
            cp.start()

    def finish(copies):
        for cp in copies:
            cp.wait()

    def swap(copies):
        begin(copies)
        finish(copies)

    class Stats:
        def __init__(self, part):
            self.part = part
            self.c1, self.c2, self.c3 = [], [], []
            for k in range(1, 8):
                p, dev = peer1(k)
                self.c1.append(remote(st.at[part, p], r1.at[part, g1], s1send.at[part, k], s1recv.at[part, k], dev))
                self.c3.append(remote(s3.at[part], r3.at[part, g1], s3send.at[part, k], s3recv.at[part, k], dev))
                p, dev = peer2(k)
                self.c2.append(remote(s2.at[part], r2.at[part, g2], s2send.at[part, k], s2recv.at[part, k], dev))

        def step1(self):
            r1[self.part, g1] = st[self.part, g1]
            begin(self.c1)

        def step2(self):
            finish(self.c1)
            put(s2, self.part, merged(r1, self.part))
            r2[self.part, g2] = s2[self.part]
            begin(self.c2)

        def step3(self):
            finish(self.c2)
            put(s3, self.part, merged(r2, self.part))
            r3[self.part, g1] = s3[self.part]
            begin(self.c3)

        def step4(self):
            finish(self.c3)
            for gi in range(8):
                st[self.part, gi, pl.ds(0, 4), :] = jnp.exp2(
                    st[self.part, gi, pl.ds(0, 4), :] - r3[self.part, gi, pl.ds(0, 4), :]
                ) / (r3[self.part, gi, pl.ds(4, 4), :] * 128.0)

    def index_stats():
        hcopy.wait()
        it = jnp.where(seen(), (ipart[...] + irecv[...]) * LOG2E, MASKED)
        im = jnp.max(it, axis=0, keepdims=True)
        il = jnp.sum(jnp.exp2(it - im), axis=0, keepdims=True)
        mis[...] = it
        for gi in range(8):
            st[0, gi, pl.ds(8, 1), :] = im
            st[0, gi, pl.ds(9, 1), :] = il

    st[...] = jnp.zeros_like(st)
    stats0, stats1 = Stats(0), Stats(1)

    prepare(0, lq)
    peak0 = scores(lq, sc)
    prepare(1, lq2)

    def two_pairs(i, peak):
        p = 2 * i
        peak2 = scores(lq2, sc2)
        prepare(jnp.minimum(p + 2, PAIRS - 1), lq)
        powers(p, sc, peak)
        nxt = scores(lq, sc)
        prepare(jnp.minimum(p + 3, PAIRS - 1), lq2)
        powers(p + 1, sc2, peak2)

        @pl.when(i == 2)
        def _():
            p2.step6()

        @pl.when(i == 6)
        def _():
            p2.step7()
            widened(hst, 6144, 176, 96)

        @pl.when(i == 7)
        def _():
            index_stats()
            stats0.step1()

        @pl.when(i == 10)
        def _():
            stats0.step2()

        @pl.when(i == 12)
        def _():
            stats0.step3()

        @pl.when(i == 15)
        def _():
            stats0.step4()

        return nxt

    lax.fori_loop(0, PAIRS // 2, two_pairs, peak0)

    def add_heads(part, ch, acc):
        def add_group(gi, acc):
            for a in range(2):
                pw = pm[part * 16 + gi * 2 + a, pl.ds(ch * TCH, TCH), :].astype(F32)
                acc = acc + pw[:, :128] * st[part, gi, pl.ds(2 * a, 1), :]
                acc = acc + pw[:, 128:] * st[part, gi, pl.ds(2 * a + 1, 1), :]
            return acc

        return lax.fori_loop(0, 8, add_group, acc, unroll=2)

    def early(chs):
        for ch in chs:
            tpart[pl.ds(ch * TCH, TCH), :] = add_heads(0, ch, jnp.zeros((TCH, QUERIES), F32))

    stats1.step1()
    early(range(0, CHUNKS // 2))
    stats1.step2()
    early(range(CHUNKS // 2, CHUNKS))
    stats1.step3()
    gqt[...] = jnp.zeros_like(gqt)
    gwt[...] = jnp.zeros_like(gwt)
    jpeak, jtotal = s3[0, pl.ds(8, 1), :], s3[0, pl.ds(9, 1), :]
    stats1.step4()

    tcopies = []
    for ch in range(CHUNKS):
        rows = pl.ds(ch * TCH, TCH)
        tpart[rows, :] = add_heads(1, ch, tpart[rows, :])
        cp = remote(tpart.at[rows], trecv.at[rows], tsend.at[ch], trsem.at[ch], at(hd_=1 - hd))
        cp.start()
        tcopies.append(cp)

    kcopies = []
    for ch in range(CHUNKS):
        rows = pl.ds(ch * TCH, TCH)
        tcopies[ch].wait()
        predicted = jnp.exp2(mis[rows, :] - jpeak) / jtotal
        mis[rows, :] = (predicted - (tpart[rows, :] + trecv[rows, :])) * ALL_KEYS

        def slope_pair(jp, acc, rows=rows):
            iq = iqs[jp]
            mf = mis[rows, :]
            d = nt(key[rows, :], iq)
            parts = []
            for e in range(2):
                de = d[:, e * 128 : e * 128 + 128]
                gwt[pl.ds(2 * jp + e, 1), :] += jnp.sum(mf * jnp.maximum(de, 0.0), axis=0, keepdims=True)
                parts.append(jnp.where(de > 0, mf * wt[pl.ds(2 * jp + e, 1), :], 0.0).astype(BF16))
            sl = jnp.concatenate(parts, axis=1)
            gqt[jp] += nn(keyt[:, rows], sl)
            return acc + nn(sl, iq)

        gkp[rows, :] = lax.fori_loop(0, IPAIRS, slope_pair, jnp.zeros((TCH, IDIM), F32), unroll=UNR)
        cp = remote(gkp.at[rows], gkr.at[rows], ksend.at[ch], krsem.at[ch], at(hd_=1 - hd))
        cp.start()
        kcopies.append(cp)

    for j in range(IHEADS):
        tr = jnp.transpose(gqt[j // 2, :, pl.ds((j % 2) * 128, 128)])
        for r in range(2):
            rs[pl.ds(r * 32 + j, 64, stride=BR), :] = tr[r * 64 : r * 64 + 64]
    tw = jnp.transpose(gwt[...]) * INDEX_SCALE
    for r in range(16):
        rs[pl.ds(64 + r, 64, stride=BR), :] = tw[r * 64 : r * 64 + 64] if r < 2 else jnp.zeros((64, 128), F32)

    ccopy = remote(
        rs.at[pl.ds(pl.multiple_of((1 - c) * 32 * BR, BR), 32 * BR)], rcv, csend, crecv, other
    )
    ccopy.start()
    ccopy.wait()

    def add_core(o, _):
        oy, ox, oz = o // 8, lax.rem(o // 2, 4), lax.rem(o, 2)
        here = pl.ds(pl.multiple_of(o * BR, BR), BR)
        v = rcv[here, :] + rs[pl.ds(pl.multiple_of((c * 32 + o) * BR, BR), BR), :]
        rcv[here, :] = v
        w = v[64:72]
        low = w - w.astype(BF16).astype(F32)
        sb[oy, ox, oz] = jnp.concatenate([v[:72], low], axis=0).astype(BF16)
        return 0

    lax.fori_loop(0, 32, add_core, 0)
    cps = []
    for k in range(1, 4):
        yp, xp = lax.rem(y + k, 4), lax.rem(x + k, 4)
        cps.append(remote(sb.at[yp, four, 0], rya.at[k], ysend.at[k], yrecv.at[k], at(y_=yp)))
        cps.append(remote(sb.at[four, xp, 1], rxb.at[k], xsend.at[k], xrecv.at[k], at(x_=xp)))
    swap(cps)

    for o in range(4):
        for dest, src, index in (
            (0, rya, (y * 4 + o) * 2),
            (1, rxb, (o * 4 + x) * 2 + 1),
        ):
            v = rcv[pl.ds(pl.multiple_of(index * BR, BR), BR), :]
            main, w = v[:64], v[64:72]
            for k in range(1, 4):
                vk = src[k, o].astype(F32)
                main, w = main + vk[:64], w + (vk[64:72] + vk[72:])
            pab[dest, o, pl.ds(0, 64), :] = main
            pab[dest, o, pl.ds(64, 8), :] = w
            pab[dest, o, pl.ds(72, 8), :] = jnp.zeros((8, 128), F32)
    mine = x * (1 - zh) + y * zh
    theirs = x * zh + y * (1 - zh)
    rz[zh * 4 + mine] = pab[zh, mine]
    cps = []
    for k in range(1, 4):
        yp, xp = lax.rem(y + k, 4), lax.rem(x + k, 4)
        slot = zh * 4 + x
        cps.append(remote(pab.at[0, xp], rz.at[slot], zsend.at[k], zrecv.at[slot], at(zh_=0, x_=xp)))
        slot = zh * 4 + y
        cps.append(remote(pab.at[1, yp], rz.at[slot], zsend.at[3 + k], zrecv.at[slot], at(zh_=1, y_=yp)))
    slot = zh * 4 + theirs
    cps.append(remote(pab.at[1 - zh, theirs], rz.at[slot], zsend.at[0], zrecv.at[slot], across))
    begin(cps)
    for cp in cps:
        cp.wait_send()
    for k in range(1, 8):
        slot = lax.rem(zh * 4 + mine + k, 8)
        remote(pab.at[0, 0], rz.at[slot], zsend.at[0], zrecv.at[slot], across).wait_recv()
    total = rz[0]
    for k in range(1, 8):
        total = total + rz[k]
    raw[pl.ds(0, BR), :] = total
    for r in range(2):
        for j in range(IHEADS):
            gq_out[pl.ds(r, 1), pl.ds(j * 128, 128)] = raw[pl.ds(r * 32 + j, 1), :]
        gw_out[pl.ds(r, 1), :] = raw[pl.ds(64 + r, 1), pl.ds(0, IHEADS)]
    for cp in kcopies:
        cp.wait()
    gk_out[...] = gkp[...] + gkr[...]


def shards(q_heads, w_uk, latent_t, index_query, index_key, head_weight, query_pos, key_start):
    vm = pl.BlockSpec(memory_space=pltpu.VMEM)
    dma = pltpu.SemaphoreType.DMA

    def v(*shape, dtype=F32):
        return pltpu.VMEM(shape, dtype)

    return pl.pallas_call(
        body,
        out_shape=(
            jax.ShapeDtypeStruct((2, IHEADS * IDIM), F32),
            jax.ShapeDtypeStruct((KEYS, IDIM), F32),
            jax.ShapeDtypeStruct((2, IHEADS), F32),
        ),
        in_specs=[vm, vm, vm, vm, vm, pl.BlockSpec(memory_space=pl.ANY), vm, vm],
        out_specs=(vm, vm, vm),
        scratch_shapes=[
            v(272, 128),
            v(8, 128, dtype=jnp.int32),
            v(8, 128, dtype=jnp.int32),
            v(2, 4, 4, 2, 272, 128, dtype=BF16),
            v(2 * 64 * 96, 128),
            v(64 * 80, 128),
            v(HEADS, NOPE, 512, dtype=BF16),
            v(KEYS, 768, dtype=BF16),
            v(256, 768, dtype=BF16),
            v(256, 768, dtype=BF16),
            v(KEYS, 256),
            v(KEYS, 256),
            v(PAIRS, KEYS, 256, dtype=BF16),
            v(IPAIRS, 256, 128, dtype=BF16),
            v(128, 128),
            v(KEYS, 128),
            v(KEYS, 128),
            v(2, 8, 16, 128),
            v(2, 8, 16, 128),
            v(2, 16, 128),
            v(2, 8, 16, 128),
            v(2, 16, 128),
            v(2, 8, 16, 128),
            v(KEYS, 128),
            v(KEYS, 128),
            v(KEYS, 128),
            v(128, KEYS, dtype=BF16),
            v(IPAIRS, 128, 256),
            v(128, 128),
            v(KEYS, 128),
            v(KEYS, 128),
            v(64 * BR, 128),
            v(32 * BR, 128),
            v(4, 4, 2, BR, 128, dtype=BF16),
            v(4, 4, BR, 128, dtype=BF16),
            v(4, 4, BR, 128, dtype=BF16),
            v(2, 4, BR, 128),
            v(8, BR, 128),
            dma, dma((NCOPY,)), dma((NCOPY,)), dma, dma,
            dma((CHUNKS,)), dma((CHUNKS,)), dma((CHUNKS,)), dma((CHUNKS,)),
            dma((2, 8)), dma((2, 8)), dma((2, 8)), dma((2, 8)), dma((2, 8)), dma((2, 8)),
            dma, dma, dma((4,)), dma((4,)), dma((4,)), dma((4,)),
            dma((8,)), dma((8,)),
        ],
        compiler_params=pltpu.CompilerParams(
            collective_id=0, has_side_effects=True, vmem_limit_bytes=63 * 1024 * 1024
        ),
    )(
        q_heads, index_query, head_weight, key_start.reshape(1, QUERIES), query_pos.reshape(1, QUERIES),
        w_uk, latent_t, index_key,
    )


def solution(mesh):
    torus = Mesh(mesh.devices.reshape(2, 4, 4, 2, 2), AXES)
    placed = (
        P(CTX, "head"),
        P("head", None, None),
        P(None, CTX),
        P(CTX, "head"),
        P(CTX, None),
        P(CTX, "head"),
        P(),
        P(),
    )
    return jax.shard_map(
        shards,
        mesh=torus,
        in_specs=placed,
        out_specs=(P(CTX, "head"), P(CTX, None), P(CTX, "head")),
        check_vma=False,
    )
```

time: 156 us -> 130 us (0.83)
  Pallas kernels: 145 us -> 125 us
  local copies, waits for them, and re-layouts: 9.4 us -> 4.44 us
    pallas_call x1, Pallas kernels: 145 us -> 125 us  [shards(): pl.pallas_call(body, out_shape=(jax.ShapeDtypeStruct((2, IHEADS * IDIM),...]
    reshape x8 -> x0, local copies, waits for them, and re-layouts: 4.3 us -> none  [the longest x4 1.93 us: ordered(): return v.reshape(2, 4, 4, 2, 2).transpose(4, 3, 1, 2, 0).reshape(1, QUERIES)]
    unnamed x1 -> x3, local copies, waits for them, and re-layouts: 1.87 us -> 4.44 us
    slice x4 -> x0, local copies, waits for them, and re-layouts: 2.01 us -> none  [the longest x1 1.24 us: shards(): grad_weight = rs[64:66, :IHEADS]]
where the time goes in v1:
time: 130 us
  Pallas kernels  125 us (96%)
  local copies, waits for them, and re-layouts  4.44 us (3%)
    pallas_call x1, Pallas kernels, shards(): pl.pallas_call(body, out_shape=(jax.ShapeDtypeStruct((2, IHEADS * IDIM),...  125 us
    unnamed x3, local copies, waits for them, and re-layouts  4.44 us

profile of v1, /device:TPU:0, one launch (start us, length us, event | category | flops | bytes accessed | tf_op | source)
XLA Modules:
  0.0 129.7 jit_solution(14078726450798498768)
XLA Ops:
  0.6 124.6 %shard_map.103 = (f32[2,4096]{1,0:T(2,128)}, f32[1024,128]{1,0:T(8,128)}, f32[2,32]{1,0:T(2,128)}) custom-call(bf16[2,12288]{1,0:T(2,128)(2,1)} %qh.1, bf16[2,4096]{1,0:T(2,128)(2,1)} %iqh.1, bf16[2,32]{1,0:T(2,128)(2,1)} %hw.1, s32[1,128]{1,0:T(1,128)} %bitcast.2, s32[1,128]{1,0:T(1,128)} %bitcast.3, bf16[64,128,512]{2,1,0:T(8,128)(2,1)} %wuk.1, ...), custom_call_target="tpu_custom_call" | custom-call | tf_op jit(solution)/shard_map/pallas_call | solution.py:563
  125.3 1.4 %copy.14 = f32[2,4096]{1,0:T(2,128)} copy(f32[2,4096]{1,0:T(2,128)} %get-tuple-element.6) | data formatting | bytes 65536
  126.6 1.9 %copy.15 = f32[1024,128]{1,0:T(8,128)} copy(f32[1024,128]{1,0:T(8,128)} %get-tuple-element.7) | data formatting | bytes 1048576
  128.5 1.2 copy.16

commit v2 on v1

--- a/solution.py
+++ b/solution.py
@@ -27,7 +27,7 @@
 TCH = 256
 CHUNKS = KEYS // TCH
 BR = 80
-NCOPY = 75
+NCOPY = 84
 UNR = 4
 SCH = 256
 
@@ -133,64 +133,46 @@
     yr, yl = lax.rem(y + 1, 4), lax.rem(y + 3, 4)
     xo, yo = lax.rem(x + 2, 4), lax.rem(y + 2, 4)
     both, four = pl.ds(0, 2), pl.ds(0, 4)
-    front, back = pl.ds(0, 2), pl.ds(2, 2)
-    dxr, dxl, dyr, dyl = at(x_=xr), at(x_=xl), at(y_=yr), at(y_=yl)
     other, across = at(c_=1 - c), at(zh_=1 - zh)
+    near = (1, 3, 2)
+    peers_zx = [at(x_=lax.rem(x + k, 4)) for k in near] + [across]
+    peers_zx += [at(zh_=1 - zh, x_=lax.rem(x + k, 4)) for k in near]
+    peers_zy = [at(y_=lax.rem(y + k, 4)) for k in near] + [across]
+    peers_zy += [at(zh_=1 - zh, y_=lax.rem(y + k, 4)) for k in near]
 
     class Piece:
         def __init__(self, row, na, nb):
             ra, rb = pl.ds(row, na), pl.ds(row + na, nb)
-            self.z = gcopy(g.at[c, y, x, zh, pl.ds(row, na + nb)], across)
-            self.a1 = [gcopy(g.at[c, y, x, both, ra], d) for d in (dxr, dxl)]
-            self.b1 = [gcopy(g.at[c, y, x, both, rb], d) for d in (dyr, dyl)]
-            self.a2 = [gcopy(g.at[c, y, xl, 0, ra], dxr), gcopy(g.at[c, y, xr, 1, ra], dxl)]
-            self.b2 = [gcopy(g.at[c, yl, x, 0, rb], dyr), gcopy(g.at[c, yr, x, 1, rb], dyl)]
-            self.a3 = [gcopy(g.at[c, y, four, both, ra], d) for d in (dyr, dyl)]
-            self.b3 = [gcopy(g.at[c, four, x, both, rb], d) for d in (dxr, dxl)]
-            self.a4 = [gcopy(g.at[c, yl, front, both, ra], dyr), gcopy(g.at[c, yr, back, both, ra], dyl)]
-            self.b4 = [gcopy(g.at[c, front, xl, both, rb], dxr), gcopy(g.at[c, back, xr, both, rb], dxl)]
-            self.ca = [gcopy(g.at[c, yy, four, both, ra], other) for yy in (y, yl, yr, yo)]
-            self.cb = [gcopy(g.at[c, four, xx, both, rb], other) for xx in (x, xl, xr, xo)]
+            own_a, own_b = g.at[c, y, x, zh, ra], g.at[c, y, x, zh, rb]
+            self.a1 = [gcopy(own_a, d) for d in peers_zx]
+            self.b1 = [gcopy(own_b, d) for d in peers_zy]
+            self.a2 = [gcopy(g.at[c, y, four, both, ra], at(y_=q)) for q in (yr, yl, yo)]
+            self.b2 = [gcopy(g.at[c, four, x, both, rb], at(x_=q)) for q in (xr, xl, xo)]
+            self.ca = [gcopy(g.at[c, q, four, both, ra], other) for q in (y, yl, yr, yo)]
+            self.cb = [gcopy(g.at[c, four, q, both, rb], other) for q in (x, xl, xr, xo)]
 
         def step1(self):
-            self.z.start()
-
-        def step2(self):
-            self.z.wait_recv()
             for cp in self.a1 + self.b1:
                 cp.start()
 
-        def step3(self):
-            for k in range(2):
-                for before, after in ((self.a1, self.a2), (self.b1, self.b2)):
-                    before[k].wait_recv()
-                    after[k].start()
-
-        def step4(self):
-            for before, after, core in ((self.a2, self.a3, self.ca), (self.b2, self.b3, self.cb)):
+        def step2(self):
+            for before, after, core in ((self.a1, self.a2, self.ca), (self.b1, self.b2, self.cb)):
                 for cp in before:
                     cp.wait_recv()
                 for cp in after:
                     cp.start()
                 core[0].start()
 
-        def step5(self):
-            for k in range(2):
-                for before, after, core in ((self.a3, self.a4, self.ca), (self.b3, self.b4, self.cb)):
+        def step3(self):
+            for k in range(3):
+                for before, core in ((self.a2, self.ca), (self.b2, self.cb)):
                     before[k].wait_recv()
-                    after[k].start()
                     core[1 + k].start()
 
-        def step6(self):
-            for before, core in ((self.a4, self.ca), (self.b4, self.cb)):
-                for cp in before:
-                    cp.wait_recv()
-                core[3].start()
-
-        def step7(self):
+        def step4(self):
             for cp in self.ca + self.cb:
                 cp.wait()
-            for cp in [self.z] + self.a1 + self.b1 + self.a2 + self.b2 + self.a3 + self.b3 + self.a4 + self.b4:
+            for cp in self.a1 + self.b1 + self.a2 + self.b2:
                 cp.wait_send()
 
     first = (((zh * 4 + y) * 4 + x) * 2 + c) * KEYS
@@ -207,28 +189,21 @@
     p1.step1()
     p2.step1()
     lext[:, pl.ds(640, 128)] = jnp.where(seen(), 0.0, MASKED).astype(BF16)
-    p0.step2()
     eye = (qa == qb).astype(F32).astype(BF16)
     for ref in (lq, lq2):
         ref[pl.ds(0, 128), pl.ds(640, 128)] = eye
         ref[pl.ds(128, 128), pl.ds(640, 128)] = eye
+    turn(0)
+    p0.step2()
+    turn(1)
+    turn(2)
+    turn(3)
     p1.step2()
-    turn(0)
-    p0.step3()
-    p2.step2()
-    turn(1)
-    p0.step4()
-    p1.step3()
-    turn(2)
-    p2.step3()
-    p0.step5()
-    p1.step4()
-    turn(3)
     rope_rows = lat[pl.ds(512, 64), :].astype(F32)
     lext[:, pl.ds(512, 128)] = jnp.transpose(jnp.concatenate([rope_rows, rope_rows], axis=0)).astype(BF16)
     keyt[...] = jnp.transpose(key[...].astype(F32)).astype(BF16)
-    p0.step6()
-    p0.step7()
+    p0.step3()
+    p0.step4()
 
     def widened(dest, base, row, rows):
         def one(o, _):
@@ -257,14 +232,12 @@
         return 0
 
     lax.fori_loop(0, IPAIRS // 2, index_pair, 0, unroll=2)
-    p1.step5()
-    p2.step4()
+    p1.step3()
+    p2.step2()
     lax.fori_loop(IPAIRS // 2, IPAIRS, index_pair, 0, unroll=2)
     hcopy = remote(ipart, irecv, hsend, hrecv, at(hd_=1 - hd))
     hcopy.start()
-    p1.step6()
-    p2.step5()
-    p1.step7()
+    p1.step4()
     widened(hst, 0, 80, 96)
 
     wcopy.wait()
@@ -392,11 +365,11 @@
 
         @pl.when(i == 2)
         def _():
-            p2.step6()
+            p2.step3()
 
         @pl.when(i == 6)
         def _():
-            p2.step7()
+            p2.step4()
             widened(hst, 6144, 176, 96)
 
         @pl.when(i == 7)

time: 130 us -> 122 us (0.938)
  Pallas kernels: 125 us -> 117 us
    pallas_call x1, Pallas kernels: 125 us -> 117 us  [shards(): pl.pallas_call(body, out_shape=(jax.ShapeDtypeStruct((2, IHEADS * IDIM),...]
where the time goes in v2:
time: 122 us
  Pallas kernels  117 us (96%)
  local copies, waits for them, and re-layouts  4.44 us (4%)
    pallas_call x1, Pallas kernels, shards(): pl.pallas_call(body, out_shape=(jax.ShapeDtypeStruct((2, IHEADS * IDIM),...  117 us
    unnamed x3, local copies, waits for them, and re-layouts  4.44 us

profile of v2, /device:TPU:0, one launch (start us, length us, event | category | flops | bytes accessed | tf_op | source)
XLA Modules:
  0.0 122.0 jit_solution(1563477616942637147)
XLA Ops:
  0.6 116.9 %shard_map.103 = (f32[2,4096]{1,0:T(2,128)}, f32[1024,128]{1,0:T(8,128)}, f32[2,32]{1,0:T(2,128)}) custom-call(bf16[2,12288]{1,0:T(2,128)(2,1)} %qh.1, bf16[2,4096]{1,0:T(2,128)(2,1)} %iqh.1, bf16[2,32]{1,0:T(2,128)(2,1)} %hw.1, s32[1,128]{1,0:T(1,128)} %bitcast.2, s32[1,128]{1,0:T(1,128)} %bitcast.3, bf16[64,128,512]{2,1,0:T(8,128)(2,1)} %wuk.1, ...), custom_call_target="tpu_custom_call" | custom-call | tf_op jit(solution)/shard_map/pallas_call | solution.py:536
  117.5 1.4 %copy.14 = f32[2,4096]{1,0:T(2,128)} copy(f32[2,4096]{1,0:T(2,128)} %get-tuple-element.6) | data formatting | bytes 65536
  118.9 1.9 %copy.15 = f32[1024,128]{1,0:T(8,128)} copy(f32[1024,128]{1,0:T(8,128)} %get-tuple-element.7) | data formatting | bytes 1048576
  120.8 1.2 copy.16

commit v3 on v2

--- a/solution.py
+++ b/solution.py
@@ -24,11 +24,13 @@
 SCORE_K = (NOPE + ROPE) ** -0.5 * LOG2E
 INDEX_SCALE = (IDIM * 64) ** -0.5
 MASKED = -1.0e30
-TCH = 256
-CHUNKS = KEYS // TCH
+CUTS = ((0, 256), (256, 256), (512, 256), (768, 256))
+CHUNKS = len(CUTS)
 BR = 80
 NCOPY = 84
 UNR = 4
+PUN = 4
+DCH = 1024
 SCH = 256
 
 F32 = jnp.float32
@@ -45,7 +47,7 @@
 
 def body(
     qh, iqh, hw, start_in, pos_in, wuk, lat, key, gq_out, gk_out, gw_out,
-    raw, low, high, g, hst, ist, wv, lext, lq, lq2, sc, sc2, pm, iqs, wt, ipart, irecv,
+    raw, low, high, g, hst, ist, wv, lext, rot, eyes, sc, sc2, pm, iqs, wt, ipart, irecv,
     st, r1, s2, r2, s3, r3, tpart, trecv, mis, keyt, gqt, gwt, gkp, gkr,
     rs, rcv, sb, rya, rxb, pab, rz,
     wsem, gsend, grecv, hsend, hrecv, tsend, trsem, ksend, krsem,
@@ -187,14 +189,13 @@
     p0, p1, p2 = Piece(0, 32, 48), Piece(80, 48, 48), Piece(176, 48, 48)
     p0.step1()
     p1.step1()
-    p2.step1()
     lext[:, pl.ds(640, 128)] = jnp.where(seen(), 0.0, MASKED).astype(BF16)
     eye = (qa == qb).astype(F32).astype(BF16)
-    for ref in (lq, lq2):
-        ref[pl.ds(0, 128), pl.ds(640, 128)] = eye
-        ref[pl.ds(128, 128), pl.ds(640, 128)] = eye
+    eyes[pl.ds(0, 128), :] = eye
+    eyes[pl.ds(128, 128), :] = eye
     turn(0)
     p0.step2()
+    p2.step1()
     turn(1)
     turn(2)
     turn(3)
@@ -243,28 +244,40 @@
     wcopy.wait()
     half = lax.broadcasted_iota(jnp.int32, (128, 128), 1) // 64
 
-    def prepare(p, dest):
+    def prepare(p, _):
         base = (p // 16) * 6144
         pr = lax.rem(p, 16)
         rp = rows_of(hst, base + 64 + pr, 16, 96)
         for e in range(2):
             qn = rows_of(hst, base + pr * 2 + e, 32, 96).astype(BF16)
-            dest[pl.ds(e * 128, 128), pl.ds(0, 512)] = nn(qn, wv[2 * p + e]).astype(BF16)
-            dest[pl.ds(e * 128, 128), pl.ds(512, 128)] = jnp.where(half == e, rp, 0.0).astype(BF16)
-
-    def scores(src, dest):
+            wv[2 * p + e] = nn(qn, wv[2 * p + e]).astype(BF16)
+            rot[p, pl.ds(e * 128, 128), :] = jnp.where(half == e, rp, 0.0).astype(BF16)
+        return 0
+
+    def scores(f, dest):
+        pairs = [
+            jnp.concatenate(
+                [jnp.concatenate([wv[2 * p], wv[2 * p + 1]], axis=0), rot[p], eyes[...]], axis=1
+            )
+            for p in (2 * f, 2 * f + 1)
+        ]
+        query = jnp.concatenate(pairs, axis=0)
         peak = None
-        for a in range(KEYS // SCH):
-            t = nt(lext[pl.ds(a * SCH, SCH), :], src[...])
-            dest[pl.ds(a * SCH, SCH), :] = t
-            top = jnp.max(t.reshape(SCH // 8, 8, 256), axis=0)
+        for a in range(KEYS // DCH):
+            t = nt(lext[pl.ds(a * DCH, DCH), :], query)
+            dest[pl.ds(a * DCH, DCH), :] = t
+            top = jnp.max(t.reshape(DCH // 8, 8, 512), axis=0)
             peak = top if peak is None else jnp.maximum(peak, top)
         return jnp.max(peak, axis=0, keepdims=True)
 
-    def powers(p, src, peak):
+    def powers(f, src, peaks):
+        for e in range(2):
+            powers_of(2 * f + e, src, pl.ds(e * 256, 256), peaks[:, e * 256 : e * 256 + 256])
+
+    def powers_of(p, src, cols, peak):
         total = None
         for a in range(KEYS // SCH):
-            pw = jnp.exp2((src[pl.ds(a * SCH, SCH), :] - peak) * SCORE_K)
+            pw = jnp.exp2((src[pl.ds(a * SCH, SCH), cols] - peak) * SCORE_K)
             pm[p, pl.ds(a * SCH, SCH), :] = pw.astype(BF16)
             part = jnp.sum(pw.reshape(SCH // 8, 8, 256), axis=0)
             total = part if total is None else total + part
@@ -350,53 +363,50 @@
     st[...] = jnp.zeros_like(st)
     stats0, stats1 = Stats(0), Stats(1)
 
-    prepare(0, lq)
-    peak0 = scores(lq, sc)
-    prepare(1, lq2)
-
-    def two_pairs(i, peak):
-        p = 2 * i
-        peak2 = scores(lq2, sc2)
-        prepare(jnp.minimum(p + 2, PAIRS - 1), lq)
-        powers(p, sc, peak)
-        nxt = scores(lq, sc)
-        prepare(jnp.minimum(p + 3, PAIRS - 1), lq2)
-        powers(p + 1, sc2, peak2)
-
-        @pl.when(i == 2)
+    lax.fori_loop(0, PAIRS // 2, prepare, 0, unroll=PUN)
+    peak0 = scores(0, sc)
+
+    def four_pairs(i, peak):
+        peak2 = scores(2 * i + 1, sc2)
+        powers(2 * i, sc, peak)
+        nxt = scores(jnp.minimum(2 * i + 2, PAIRS // 2 - 1), sc)
+        powers(2 * i + 1, sc2, peak2)
+
+        @pl.when(i == 0)
         def _():
             p2.step3()
 
-        @pl.when(i == 6)
+        @pl.when(i == 2)
         def _():
             p2.step4()
             widened(hst, 6144, 176, 96)
-
-        @pl.when(i == 7)
+            lax.fori_loop(PAIRS // 2, PAIRS, prepare, 0, unroll=PUN)
+
+        @pl.when(i == 3)
         def _():
             index_stats()
             stats0.step1()
 
-        @pl.when(i == 10)
+        @pl.when(i == 4)
         def _():
             stats0.step2()
 
-        @pl.when(i == 12)
+        @pl.when(i == 5)
         def _():
             stats0.step3()
 
-        @pl.when(i == 15)
+        @pl.when(i == 7)
         def _():
             stats0.step4()
 
         return nxt
 
-    lax.fori_loop(0, PAIRS // 2, two_pairs, peak0)
+    lax.fori_loop(0, PAIRS // 4, four_pairs, peak0)
 
     def add_heads(part, ch, acc):
         def add_group(gi, acc):
             for a in range(2):
-                pw = pm[part * 16 + gi * 2 + a, pl.ds(ch * TCH, TCH), :].astype(F32)
+                pw = pm[part * 16 + gi * 2 + a, pl.ds(*CUTS[ch]), :].astype(F32)
                 acc = acc + pw[:, :128] * st[part, gi, pl.ds(2 * a, 1), :]
                 acc = acc + pw[:, 128:] * st[part, gi, pl.ds(2 * a + 1, 1), :]
             return acc
@@ -405,12 +415,12 @@
 
     def early(chs):
         for ch in chs:
-            tpart[pl.ds(ch * TCH, TCH), :] = add_heads(0, ch, jnp.zeros((TCH, QUERIES), F32))
+            tpart[pl.ds(*CUTS[ch]), :] = add_heads(0, ch, jnp.zeros((CUTS[ch][1], QUERIES), F32))
 
     stats1.step1()
-    early(range(0, CHUNKS // 2))
+    early(range(0, 2))
     stats1.step2()
-    early(range(CHUNKS // 2, CHUNKS))
+    early(range(2, CHUNKS))
     stats1.step3()
     gqt[...] = jnp.zeros_like(gqt)
     gwt[...] = jnp.zeros_like(gwt)
@@ -419,7 +429,7 @@
 
     tcopies = []
     for ch in range(CHUNKS):
-        rows = pl.ds(ch * TCH, TCH)
+        rows = pl.ds(*CUTS[ch])
         tpart[rows, :] = add_heads(1, ch, tpart[rows, :])
         cp = remote(tpart.at[rows], trecv.at[rows], tsend.at[ch], trsem.at[ch], at(hd_=1 - hd))
         cp.start()
@@ -427,7 +437,7 @@
 
     kcopies = []
     for ch in range(CHUNKS):
-        rows = pl.ds(ch * TCH, TCH)
+        rows = pl.ds(*CUTS[ch])
         tcopies[ch].wait()
         predicted = jnp.exp2(mis[rows, :] - jpeak) / jtotal
         mis[rows, :] = (predicted - (tpart[rows, :] + trecv[rows, :])) * ALL_KEYS
@@ -445,7 +455,7 @@
             gqt[jp] += nn(keyt[:, rows], sl)
             return acc + nn(sl, iq)
 
-        gkp[rows, :] = lax.fori_loop(0, IPAIRS, slope_pair, jnp.zeros((TCH, IDIM), F32), unroll=UNR)
+        gkp[rows, :] = lax.fori_loop(0, IPAIRS, slope_pair, jnp.zeros((CUTS[ch][1], IDIM), F32), unroll=UNR)
         cp = remote(gkp.at[rows], gkr.at[rows], ksend.at[ch], krsem.at[ch], at(hd_=1 - hd))
         cp.start()
         kcopies.append(cp)
@@ -526,6 +536,12 @@
     gk_out[...] = gkp[...] + gkr[...]
 
 
+def handed_on(*refs):
+    count = len(refs) // 2
+    for k in range(count):
+        refs[count + k][...] = refs[k][...]
+
+
 def shards(q_heads, w_uk, latent_t, index_query, index_key, head_weight, query_pos, key_start):
     vm = pl.BlockSpec(memory_space=pltpu.VMEM)
     dma = pltpu.SemaphoreType.DMA
@@ -533,7 +549,7 @@
     def v(*shape, dtype=F32):
         return pltpu.VMEM(shape, dtype)
 
-    return pl.pallas_call(
+    results = pl.pallas_call(
         body,
         out_shape=(
             jax.ShapeDtypeStruct((2, IHEADS * IDIM), F32),
@@ -551,10 +567,10 @@
             v(64 * 80, 128),
             v(HEADS, NOPE, 512, dtype=BF16),
             v(KEYS, 768, dtype=BF16),
-            v(256, 768, dtype=BF16),
-            v(256, 768, dtype=BF16),
-            v(KEYS, 256),
-            v(KEYS, 256),
+            v(PAIRS, 256, 128, dtype=BF16),
+            v(256, 128, dtype=BF16),
+            v(KEYS, 512),
+            v(KEYS, 512),
             v(PAIRS, KEYS, 256, dtype=BF16),
             v(IPAIRS, 256, 128, dtype=BF16),
             v(128, 128),
@@ -594,6 +610,12 @@
         q_heads, index_query, head_weight, key_start.reshape(1, QUERIES), query_pos.reshape(1, QUERIES),
         w_uk, latent_t, index_key,
     )
+    return pl.pallas_call(
+        handed_on,
+        out_shape=tuple(jax.ShapeDtypeStruct(v.shape, v.dtype) for v in results),
+        in_specs=[vm] * 3,
+        out_specs=(vm,) * 3,
+    )(*results)
 
 
 def solution(mesh):

time: 122 us -> 118 us (0.967)
  local copies, waits for them, and re-layouts: 4.44 us -> 0 us
    unnamed x3 -> x0, local copies, waits for them, and re-layouts: 4.44 us -> none
    pallas_call x0 -> x1, Pallas kernels: none -> 1.87 us  [shards(): pl.pallas_call(handed_on, out_shape=tuple((jax.ShapeDtypeStruct(v.shape,...]
where the time goes in v3:
time: 118 us
  Pallas kernels  118 us (100%)
    pallas_call x1, Pallas kernels, shards(): pl.pallas_call(body, out_shape=(jax.ShapeDtypeStruct((2, IHEADS * IDIM),...  116 us

profile of v3, /device:TPU:0, one launch (start us, length us, event | category | flops | bytes accessed | tf_op | source)
XLA Modules:
  0.0 118.2 jit_solution(8808457863386699913)
XLA Ops:
  0.6 115.7 %shard_map.103 = (f32[2,4096]{1,0:T(2,128)}, f32[1024,128]{1,0:T(8,128)}, f32[2,32]{1,0:T(2,128)}) custom-call(bf16[2,12288]{1,0:T(2,128)(2,1)} %qh.1, bf16[2,4096]{1,0:T(2,128)(2,1)} %iqh.1, bf16[2,32]{1,0:T(2,128)(2,1)} %hw.1, s32[1,128]{1,0:T(1,128)} %bitcast.2, s32[1,128]{1,0:T(1,128)} %bitcast.3, bf16[64,128,512]{2,1,0:T(8,128)(2,1)} %wuk.1, ...), custom_call_target="tpu_custom_call" | custom-call | tf_op jit(solution)/shard_map/pallas_call | solution.py:552
  116.3 1.9 %shard_map.104 = (f32[2,4096]{1,0:T(2,128)}, f32[1024,128]{1,0:T(8,128)}, f32[2,32]{1,0:T(2,128)}) custom-call(f32[2,4096]{1,0:T(2,128)} %get-tuple-element.6.refs_0_, f32[1024,128]{1,0:T(8,128)} %get-tuple-element.7.refs_1_, f32[2,32]{1,0:T(2,128)} %get-tuple-element.8.refs_2_), custom_call_target="tpu_custom_call" | custom-call | tf_op jit(solution)/shard_map/pallas_call | solution.py:613

commit v4 on v3

--- a/solution.py
+++ b/solution.py
@@ -24,12 +24,12 @@
 SCORE_K = (NOPE + ROPE) ** -0.5 * LOG2E
 INDEX_SCALE = (IDIM * 64) ** -0.5
 MASKED = -1.0e30
-CUTS = ((0, 256), (256, 256), (512, 256), (768, 256))
+CUTS = ((0, 256), (256, 256), (512, 512))
 CHUNKS = len(CUTS)
 BR = 80
 NCOPY = 84
-UNR = 4
-PUN = 4
+UNR = 8
+PUN = 8
 DCH = 1024
 SCH = 256
 
@@ -232,10 +232,10 @@
         ipart[...] += d[:, :128] * w0 + d[:, 128:] * w1
         return 0
 
-    lax.fori_loop(0, IPAIRS // 2, index_pair, 0, unroll=2)
+    lax.fori_loop(0, IPAIRS // 2, index_pair, 0, unroll=4)
     p1.step3()
     p2.step2()
-    lax.fori_loop(IPAIRS // 2, IPAIRS, index_pair, 0, unroll=2)
+    lax.fori_loop(IPAIRS // 2, IPAIRS, index_pair, 0, unroll=4)
     hcopy = remote(ipart, irecv, hsend, hrecv, at(hd_=1 - hd))
     hcopy.start()
     p1.step4()
@@ -411,7 +411,7 @@
                 acc = acc + pw[:, 128:] * st[part, gi, pl.ds(2 * a + 1, 1), :]
             return acc
 
-        return lax.fori_loop(0, 8, add_group, acc, unroll=2)
+        return lax.fori_loop(0, 8, add_group, acc, unroll=4)
 
     def early(chs):
         for ch in chs:

time: 118 us -> 115 us (0.975)
  Pallas kernels: 118 us -> 114 us
    pallas_call x1, Pallas kernels: 116 us -> 112 us  [shards(): pl.pallas_call(body, out_shape=(jax.ShapeDtypeStruct((2, IHEADS * IDIM),...]
where the time goes in v4:
time: 115 us
  Pallas kernels  114 us (99%)
    pallas_call x1, Pallas kernels, shards(): pl.pallas_call(body, out_shape=(jax.ShapeDtypeStruct((2, IHEADS * IDIM),...  112 us

profile of v4, /device:TPU:0, one launch (start us, length us, event | category | flops | bytes accessed | tf_op | source)
XLA Modules:
  0.0 114.7 jit_solution(1383125401898766213)
XLA Ops:
  0.6 112.2 %shard_map.103 = (f32[2,4096]{1,0:T(2,128)}, f32[1024,128]{1,0:T(8,128)}, f32[2,32]{1,0:T(2,128)}) custom-call(bf16[2,12288]{1,0:T(2,128)(2,1)} %qh.1, bf16[2,4096]{1,0:T(2,128)(2,1)} %iqh.1, bf16[2,32]{1,0:T(2,128)(2,1)} %hw.1, s32[1,128]{1,0:T(1,128)} %bitcast.2, s32[1,128]{1,0:T(1,128)} %bitcast.3, bf16[64,128,512]{2,1,0:T(8,128)(2,1)} %wuk.1, ...), custom_call_target="tpu_custom_call" | custom-call | tf_op jit(solution)/shard_map/pallas_call | solution.py:552
  112.8 1.9 %shard_map.104 = (f32[2,4096]{1,0:T(2,128)}, f32[1024,128]{1,0:T(8,128)}, f32[2,32]{1,0:T(2,128)}) custom-call(f32[2,4096]{1,0:T(2,128)} %get-tuple-element.6.refs_0_, f32[1024,128]{1,0:T(8,128)} %get-tuple-element.7.refs_1_, f32[2,32]{1,0:T(2,128)} %get-tuple-element.8.refs_2_), custom_call_target="tpu_custom_call" | custom-call | tf_op jit(solution)/shard_map/pallas_call | solution.py:613
